TPU v7x, 128 devices: a whole 4x4x4 slice. The times are simulated.
128 devices in a mesh: patch: 64 (over x, z, y_lo, core), head: 2 (over y_hi).
Axes of the slice: x: 4, y: 4 (y_hi: 2, y_lo: 2; y = y_hi * 2 + y_lo), z: 4, core: 2. Of those that a mesh axis runs over, the one named last changes fastest.
Arguments:
- hidden: bfloat16 [2, 12288, 3072], P(None, ('patch', 'head')), may hold values from -2.5 to 2.5
- queries: bfloat16 [2, 12288, 1536], P(None, ('patch', 'head')), may hold values from -8 to 8
- keys: bfloat16 [2, 12288, 1536], P(None, ('patch', 'head')), may hold values from -8 to 8
- values: bfloat16 [2, 12288, 1536], P(None, ('patch', 'head')), may hold values from -6 to 6
- out_weight: bfloat16 [1536, 3072], replicated, may hold values from -0.15625 to 0.15625
- gate_table: float32 [50, 3072], replicated, may hold values from -4 to 4
- steps_t: int32 [2], replicated, may hold values from 0 to 49
Outputs:
- blocked: bfloat16 [2, 12288, 3072], P(None, ('patch', 'head'))
All inputs are finite; a program needn't handle non-finite values.
Results may differ from a plain program's by a relative error of at most 0.008.
Values may be sent and summed in bfloat16 or wider, within the bound.
A program may use at most 192 MiB of HBM per device.

v0:
```python
import math

import jax
import jax.numpy as jnp
from jax import lax
from jax.sharding import PartitionSpec as P

HD = 128


def absorb(running, query_heads, key_block, value_block):
    top_score, weight_sum, weighted = running
    block_rows = key_block.shape[0]
    heads_dev = query_heads.shape[1]
    key_heads = key_block.reshape(block_rows, heads_dev, HD)
    value_heads = value_block.reshape(block_rows, heads_dev, HD)
    scores = jnp.einsum(
        "qhd,khd->hqk", query_heads, key_heads, preferred_element_type=jnp.float32
    ) * (1.0 / math.sqrt(HD))
    new_top = jnp.maximum(top_score, jnp.max(scores, axis=-1))
    rescale = jnp.exp(top_score - new_top)
    lifted = jnp.exp(scores - new_top[:, :, None])
    weight_sum = weight_sum * rescale + jnp.sum(lifted, axis=-1)
    weighted = weighted * rescale[:, :, None] + jnp.einsum(
        "hqk,khd->hqd", lifted.astype(jnp.bfloat16), value_heads, preferred_element_type=jnp.float32
    )
    return (new_top, weight_sum, weighted)


def fresh_start(query_heads):
    group_rows = query_heads.shape[0]
    heads_dev = query_heads.shape[1]
    return (
        jnp.full((heads_dev, group_rows), -1e30, jnp.float32),
        jnp.zeros((heads_dev, group_rows), jnp.float32),
        jnp.zeros((heads_dev, group_rows, HD), jnp.float32),
    )


def sweep(running, query_heads, key_table, value_table, block_rows):
    block_count = key_table.shape[0] // block_rows

    def visit(block_id, inner):
        offset = block_id * block_rows
        key_block = lax.dynamic_slice_in_dim(key_table, offset, block_rows, 0)
        value_block = lax.dynamic_slice_in_dim(value_table, offset, block_rows, 0)
        return absorb(inner, query_heads, key_block, value_block)

    return lax.fori_loop(0, block_count, visit, running)


def settle(running, group_rows):
    top_score, weight_sum, weighted = running
    result = weighted / weight_sum[:, :, None]
    return jnp.transpose(result, (1, 0, 2)).reshape(group_rows, -1).astype(jnp.bfloat16)


def regroup(queries, keys, values, step_id, head_count, tok_rows):
    query_split = queries[step_id].reshape(tok_rows, head_count, -1)
    key_split = keys[step_id].reshape(tok_rows, head_count, -1)
    value_split = values[step_id].reshape(tok_rows, head_count, -1)
    moved = (
        lax.all_to_all(query_split, "head", split_axis=1, concat_axis=0, tiled=True),
        lax.all_to_all(key_split, "head", split_axis=1, concat_axis=0, tiled=True),
        lax.all_to_all(value_split, "head", split_axis=1, concat_axis=0, tiled=True),
    )
    return tuple((piece.reshape(piece.shape[0], -1) for piece in moved))


def finish(attended, hidden_rows, gate_row, out_weight):
    merged = lax.all_to_all(attended, "head", split_axis=0, concat_axis=1, tiled=True)
    projected = jnp.dot(merged, out_weight, preferred_element_type=jnp.float32)
    return (hidden_rows.astype(jnp.float32) + gate_row[None, :] * projected).astype(jnp.bfloat16)


def shards(hidden, queries, keys, values, out_weight, gate_table, steps_t):
    head_count = lax.axis_size("head")
    tok_rows = hidden.shape[1]
    group_rows = tok_rows * head_count
    block_rows = 8 * group_rows
    table_ids = jnp.arange(gate_table.shape[0], dtype=jnp.int32)
    picks = (table_ids[None, :] == steps_t[:, None]).astype(jnp.float32)
    gate_rows = jnp.sum(picks[:, :, None] * gate_table[None, :, :], axis=1)
    first_q, first_k, first_v = regroup(queries, keys, values, 0, head_count, tok_rows)
    query_heads = first_q.reshape(group_rows, -1, HD)
    running = fresh_start(query_heads)
    key_table, value_table = (
        lax.all_gather(first_k, "patch", axis=0, tiled=True),
        lax.all_gather(first_v, "patch", axis=0, tiled=True),
    )
    running = sweep(running, query_heads, key_table, value_table, block_rows)
    first_out = finish(settle(running, group_rows), hidden[0], gate_rows[0], out_weight)
    second_q, second_k, second_v = regroup(queries, keys, values, 1, head_count, tok_rows)
    second_heads = second_q.reshape(group_rows, -1, HD)
    own_start = lax.axis_index("patch") * group_rows
    key_patched = lax.dynamic_update_slice_in_dim(key_table, second_k, own_start, 0)
    value_patched = lax.dynamic_update_slice_in_dim(value_table, second_v, own_start, 0)
    running = sweep(fresh_start(second_heads), second_heads, key_patched, value_patched, block_rows)
    second_out = finish(settle(running, group_rows), hidden[1], gate_rows[1], out_weight)
    return jnp.stack([first_out, second_out])


def solution(mesh):
    placed = (
        P(None, ("patch", "head"), None),
        P(None, ("patch", "head"), None),
        P(None, ("patch", "head"), None),
        P(None, ("patch", "head"), None),
        P(),
        P(),
        P(),
    )
    return jax.shard_map(
        shards,
        mesh=mesh,
        in_specs=placed,
        out_specs=P(None, ("patch", "head"), None),
        check_vma=False,
    )
```

profile of v0, /device:TPU:1, one launch (start us, length us, event | category | flops | bytes accessed | tf_op | source)
XLA Modules:
  0.0 573.1 jit_solution(10484001131353486955)
XLA Ops:
  7.8 11.0 %all_to_all.122 = bf16[96,2,768]{2,0,1:T(8,128)(2,1)} all-to-all(bf16[96,2,768]{2,0,1:T(8,128)(2,1)S(1)} %copy.88), channel_id=1, replica_groups=mesh['patch'=64,'head'=2] {'head'}, dimensions={1} | all-to-all | bytes 589824 | tf_op jit(solution)/shard_map/all_to_all | solution.py:64
  20.1 8.8 %all_to_all.123 = bf16[96,2,768]{2,0,1:T(8,128)(2,1)} all-to-all(bf16[96,2,768]{2,0,1:T(8,128)(2,1)S(1)} %copy.90), channel_id=1, replica_groups=mesh['patch'=64,'head'=2] {'head'}, dimensions={1} | all-to-all | bytes 589824 | tf_op jit(solution)/shard_map/all_to_all | solution.py:65
  30.9 3.4 all-to-all-start.1
  37.0 3.1 all-to-all-done.1
  40.1 3.5 all-to-all-start.5
  45.8 3.4 all-to-all-done.5
  49.2 4.1 all-to-all-start.6
  54.5 96.9 %all-gather.3.cloned.1.call-done = bf16[12288,768]{1,0:T(8,128)(2,1)} async-done(((bf16[192,768]{1,0:T(8,128)(2,1)}), bf16[12288,768]{1,0:T(8,128)(2,1)}) %all-gather.3.cloned.1.call-update) | async-done | bytes 18874384 | tf_op jit(solution)/shard_map/all_gather | solution.py:88
  151.4 126.7 %all-gather.5.cloned.1.call-done = bf16[12288,768]{1,0:T(8,128)(2,1)} async-done(((bf16[192,768]{1,0:T(8,128)(2,1)}), bf16[12288,768]{1,0:T(8,128)(2,1)}) %all-gather.5.cloned.1.call-update) | async-done | bytes 18874384 | tf_op jit(solution)/shard_map/all_gather | solution.py:89
  278.0 125.1 %while.36 = (s32[]{:T(128)}, f32[6,192]{1,0:T(8,128)S(1)}, f32[6,192]{1,0:T(8,128)}, f32[6,192,128]{2,1,0:T(8,128)S(1)}, bf16[12288,768]{1,0:T(8,128)(2,1)}, /*i...) while((s32[]{:T(128)}, f32[6,192]{1,0:T(8,128)S(1)}, ...), condition=%wide.region_4.0_spmd.clone, body=%wide.region_1.0_spmd.clone.sunk | while | flops 920573568 | bytes 46412008 | solution.py:49
  278.0 4.1 constant_dynamic-slice_fusion.6
  284.5 2.8 copy.119
  287.4 2.9 bitcast_reduce_fusion.4
  293.7 4.1 constant_dynamic-slice_fusion.6
  300.2 2.8 copy.119
  303.0 2.9 bitcast_reduce_fusion.4
  309.3 4.1 constant_dynamic-slice_fusion.6
  315.8 2.8 copy.119
  318.7 2.9 bitcast_reduce_fusion.4
  325.0 4.1 constant_dynamic-slice_fusion.6
  331.5 2.8 copy.119
  334.3 2.9 bitcast_reduce_fusion.4
  340.6 4.1 constant_dynamic-slice_fusion.6
  347.1 2.8 copy.119
  350.0 2.9 bitcast_reduce_fusion.4
  356.2 4.1 constant_dynamic-slice_fusion.6
  362.7 2.8 copy.119
  365.6 2.9 bitcast_reduce_fusion.4
  371.9 4.1 constant_dynamic-slice_fusion.6
  378.4 2.8 copy.119
  381.2 2.9 bitcast_reduce_fusion.4
  387.5 4.1 constant_dynamic-slice_fusion.6
  394.0 2.8 copy.119
  396.9 2.9 bitcast_reduce_fusion.4
  403.2 3.8 all-to-all-start.4
  413.5 3.6 all-to-all-start.3
  417.9 124.3 %while.37 = (s32[]{:T(128)}, f32[6,192]{1,0:T(8,128)S(1)}, f32[6,192]{1,0:T(8,128)}, f32[6,192,128]{2,1,0:T(8,128)S(1)}, bf16[12288,768]{1,0:T(8,128)(2,1)}, /*i...) while((s32[]{:T(128)}, f32[6,192]{1,0:T(8,128)S(1)}, ...), condition=%wide.region_8.0_spmd.clone, body=%wide.region_5.0_spmd.clone.sunk | while | flops 920573568 | bytes 47591684 | solution.py:49
  417.9 4.1 constant_dynamic-slice_fusion.7
  424.4 2.8 copy.121
  427.3 2.8 bitcast_reduce_fusion.5
  433.4 4.1 constant_dynamic-slice_fusion.7
  439.9 2.8 copy.121
  442.8 2.8 bitcast_reduce_fusion.5
  449.0 4.1 constant_dynamic-slice_fusion.7
  455.5 2.8 copy.121
  458.3 2.8 bitcast_reduce_fusion.5
  464.5 4.1 constant_dynamic-slice_fusion.7
  471.0 2.8 copy.121
  473.9 2.8 bitcast_reduce_fusion.5
  480.1 4.1 constant_dynamic-slice_fusion.7
  486.6 2.8 copy.121
  489.4 2.8 bitcast_reduce_fusion.5
  495.6 4.1 constant_dynamic-slice_fusion.7
  502.1 2.8 copy.121
  505.0 2.8 bitcast_reduce_fusion.5
  511.1 4.1 constant_dynamic-slice_fusion.7
  517.6 2.8 copy.121
  520.5 2.8 bitcast_reduce_fusion.5
  526.7 4.1 constant_dynamic-slice_fusion.7
  533.2 2.8 copy.121
  544.4 4.0 all-to-all-start.7
  549.3 4.8 all-to-all-done.7
  554.2 5.5 fusion.28
  559.7 5.5 fusion.29
  (229 shorter events, 116.2 us)
Async XLA Ops:
  6.5 30.4 %copy-start.7 = (s32[2]{0:T(128)S(1)}, s32[2]{0:T(128)}, u32[]{:S(2)}) copy-start(s32[2]{0:T(128)} %param.17) | copy-start | bytes 28
  6.5 37.0 %copy-start.2 = (f32[50,3072]{1,0:T(8,128)S(1)}, f32[50,3072]{1,0:T(8,128)}, u32[]{:S(2)}) copy-start(f32[50,3072]{1,0:T(8,128)} %param.16) | copy-start | bytes 1843204
  6.5 144.8 %all-gather.3.cloned.1.call-start = ((), (), s32[]{:S(2)}) async-start(), calls=%async_computation.8 | async-start | bytes 19169280 | tf_op jit(solution)/shard_map/all_gather | solution.py:88
  18.9 259.2 %all-gather.5.cloned.1.call-start = ((), (), s32[]{:S(2)}) async-start(), calls=%async_computation.9 | async-start | bytes 19169280 | tf_op jit(solution)/shard_map/all_gather | solution.py:89
  30.9 9.1 %all-to-all-start.1 = ((bf16[96,2,768]{2,0,1:T(8,128)(2,1)}), bf16[96,2,768]{2,0,1:T(8,128)(2,1)S(1)}, u32[]{:S(2)}, u32[]{:S(2)}) async-start(bf16[96,2,768]{2,0,1:T(8,128)(2,1)} %copy.89), calls=%async_computation.1 | async-start | bytes 589824 | tf_op jit(solution)/shard_map/all_to_all | solution.py:63
  40.1 9.2 %all-to-all-start.5 = ((bf16[96,2,768]{2,0,1:T(8,128)(2,1)}), bf16[96,2,768]{2,0,1:T(8,128)(2,1)S(1)}, u32[]{:S(2)}, u32[]{:S(2)}) async-start(bf16[96,2,768]{2,0,1:T(8,128)(2,1)} %copy.97), calls=%async_computation.5 | async-start | bytes 589824 | tf_op jit(solution)/shard_map/all_to_all | solution.py:63
  49.2 354.0 %all-to-all-start.6 = ((bf16[96,2,768]{2,0,1:T(8,128)(2,1)}), bf16[96,2,768]{2,0,1:T(8,128)(2,1)}, u32[]{:S(2)}, u32[]{:S(2)}) async-start(bf16[96,2,768]{2,0,1:T(8,128)(2,1)} %copy.98), calls=%async_computation.6 | async-start | bytes 589824 | tf_op jit(solution)/shard_map/all_to_all | solution.py:65
  287.4 4.3 copy-start.5
  291.7 2.0 copy-start.6
  303.0 4.3 copy-start.5
  307.3 2.0 copy-start.6
  318.7 4.3 copy-start.5
  323.0 2.0 copy-start.6
  334.3 4.3 copy-start.5
  338.6 2.0 copy-start.6
  349.9 4.3 copy-start.5
  354.3 2.0 copy-start.6
  365.6 4.3 copy-start.5
  369.9 2.0 copy-start.6
  381.2 4.3 copy-start.5
  385.5 2.0 copy-start.6
  396.9 4.3 copy-start.5
  401.2 2.0 copy-start.6
  403.2 10.4 %all-to-all-start.4 = ((bf16[96,2,768]{2,0,1:T(8,128)(2,1)}), bf16[96,2,768]{2,0,1:T(8,128)(2,1)S(1)}, u32[]{:S(2)}, u32[]{:S(2)}) async-start(bf16[96,2,768]{2,0,1:T(8,128)(2,1)} %copy.96), calls=%async_computation.4 | async-start | bytes 589824 | tf_op jit(solution)/shard_map/all_to_all | solution.py:64
  413.5 130.9 %all-to-all-start.3 = ((bf16[2,96,768]{2,1,0:T(8,128)(2,1)}), bf16[2,96,768]{2,1,0:T(8,128)(2,1)S(1)}, u32[]{:S(2)}, u32[]{:S(2)}) async-start(bf16[2,96,768]{2,1,0:T(8,128)(2,1)} %convert_element_type.64), calls=%async_computation.3 | async-start | bytes 589824 | tf_op jit(solution)/shard_map/all_to_all | solution.py:71
  422.0 5.3 copy-start
  427.3 4.2 copy-start.3
  431.5 2.0 copy-start.4
  437.5 5.3 copy-start
  442.8 4.2 copy-start.3
  447.0 2.0 copy-start.4
  453.0 5.3 copy-start
  458.3 4.2 copy-start.3
  462.5 2.0 copy-start.4
  468.6 5.3 copy-start
  473.9 4.2 copy-start.3
  478.1 2.0 copy-start.4
  484.1 5.3 copy-start
  489.4 4.2 copy-start.3
  493.6 2.0 copy-start.4
  499.7 5.3 copy-start
  505.0 4.2 copy-start.3
  509.2 2.0 copy-start.4
  515.2 5.3 copy-start
  520.5 4.2 copy-start.3
  524.7 2.0 copy-start.4
  530.8 5.3 copy-start
  536.0 4.2 copy-start.3
  540.2 2.0 copy-start.4
  544.4 9.7 %all-to-all-start.7 = ((bf16[2,96,768]{2,1,0:T(8,128)(2,1)}), bf16[2,96,768]{2,1,0:T(8,128)(2,1)S(1)}, u32[]{:S(2)}, u32[]{:S(2)}) async-start(bf16[2,96,768]{2,1,0:T(8,128)(2,1)} %convert_element_type.70), calls=%async_computation.7 | async-start | bytes 589824 | tf_op jit(solution)/shard_map/all_to_all | solution.py:71
  554.2 5.5 copy-start.1
Sparse Core Ops, SparseCore 0:
  19.0 132.3 all-gather.2
  153.1 124.9 all-gather.4
where the time goes:
time: 577 us; the launch traced here: 573 us
  waiting for transfers between devices  238 us (41%)
  local copies, waits for them, and re-layouts  165 us (29%)
  matrix products  87.8 us (15%)
  other arithmetic  25.6 us (4%)
  starting transfers between devices  22.5 us (4%)
  blocking collectives  19.8 us (3%)
  between operations  13.7 us (2%)
    all_gather x1, waiting for transfers between devices, shards(): lax.all_gather(first_v, 'patch', axis=0, tiled=True)  127 us
    dynamic_slice x32, local copies, waits for them, and re-layouts, visit(): value_block = lax.dynamic_slice_in_dim(value_table, offset, block_rows, 0)  110 us
    all_gather x1, waiting for transfers between devices, shards(): lax.all_gather(first_k, 'patch', axis=0, tiled=True)  96.9 us
    dot_general x16, matrix products, absorb(): jnp.einsum('qhd,khd->hqk', query_heads, key_heads, preferred_element_type...  46 us
    dynamic_slice x16, local copies, waits for them, and re-layouts, visit(): key_block = lax.dynamic_slice_in_dim(key_table, offset, block_rows, 0)  39 us
    dot_general x16, matrix products, absorb(): jnp.einsum('hqk,khd->hqd', lifted.astype(jnp.bfloat16), value_heads, pref...  30.8 us
    reduce_sum x16, other arithmetic, absorb(): weight_sum = weight_sum * rescale + jnp.sum(lifted, axis=-1)  21.1 us
  transfers between devices with their start and end apart: 8, of which 6 were waited for; matrix products, arithmetic and copies ran while one was open for 46% of the time, Pallas kernels for 0%

commit v1 on v0

v1 whole, which is shorter than its diff:
```python
import functools
import math

import jax
import jax.numpy as jnp
from jax import lax
from jax.experimental import pallas as pl
from jax.experimental.pallas import tpu as pltpu
from jax.sharding import PartitionSpec as P

HD = 128
TOK = 96
CHUNK = 4 * TOK
QUERIES = 2 * CHUNK
RING = 4
SLOTS = 3
TILE = 256
LOG2_SCALE = math.log2(math.e) / math.sqrt(HD)
LOWEST = -1e30

SPREAD = ("y", "x", "z")
PLANE = (("x", "z"), ("y", "z"), ("y", "x"))

VISITS = (
    (1, 0), (3, 0), (0, 1), (0, 3), (1, 1), (3, 3), (1, 3), (3, 1),
    (0, 2), (2, 1), (1, 2), (2, 3), (3, 2), (2, 2),
)
PARTNER = (2, 0)

ARRIVALS = {
    0: ((1, 0), (0, 1)),
    1: ((3, 0), (0, 3)),
    2: ((2, 0), (1, 1), (1, 3)),
    3: ((3, 1), (3, 3)),
    4: ((0, 2),),
    5: ((2, 1), (2, 3)),
    7: ((1, 2), (3, 2)),
    9: ((2, 2),),
}


def block_of(index):
    return sum((index >= edge * TOK).astype(jnp.int32) for edge in range(1, RING))


def kernel(
    hidden, queries, keys, values, weight, gates, steps, out,
    kv, kv1, v_in, v1_in, q_in, qt, acc, top, total, o_out, att, w_buf, g_buf, h_buf,
    ex_send, ex_recv, ag_send, ag_recv, sib_recv, ret_send, ret_recv, local,
):
    patch, head = lax.axis_index("patch"), lax.axis_index("head")
    core = lax.rem(patch, 2)
    at = {
        "x": patch // 16,
        "z": lax.rem(patch // 4, RING),
        "y": head * 2 + lax.rem(patch // 2, 2),
    }

    def device(**moved):
        pos = dict(at, core=core)
        pos.update(moved)
        y = pos["y"]
        return (((pos["x"] * RING + pos["z"]) * 2 + lax.rem(y, 2)) * 2 + pos["core"], y // 2)

    def shifted(axis, step):
        return lax.rem(at[axis] + step, RING)

    def pick(first, second):
        return first + core * (second - first)

    def routed(s, which, step):
        a, b = PLANE[s] if which == 0 else PLANE[s][::-1]
        da, db = device(**{a: shifted(a, step)}), device(**{b: shifted(b, step)})
        return (pick(da[0], db[0]), pick(da[1], db[1]))

    def chip_at(s, da, db):
        a, b = PLANE[s]
        return shifted(a, da) * RING + shifted(b, db)

    def chip_routed(s, first, second):
        return pick(chip_at(s, first, second), chip_at(s, second, first))

    sibling = device(core=1 - core)
    far_y = shifted("y", 2)

    peers = [device(**{axis: shifted(axis, step)}) for axis in "xyz" for step in (1, 2, 3)]
    peers += [device(y=far_y, **{axis: shifted(axis, step)}) for axis in "xz" for step in (1, 2, 3)]
    peers.append(sibling)
    barrier = pltpu.get_barrier_semaphore()
    for peer in peers:
        pl.semaphore_signal(barrier, inc=1, device_id=peer, device_id_type=pl.DeviceIdType.MESH)
    pl.semaphore_wait(barrier, len(peers))

    sent, gathered = [], []

    def remote(src, dst, send_sem, recv_sem, target, start=True):
        copy = pltpu.make_async_remote_copy(
            src_ref=src, dst_ref=dst, send_sem=send_sem, recv_sem=recv_sem,
            device_id=target, device_id_type=pl.DeviceIdType.MESH,
        )
        if start:
            copy.start()
        return copy

    def rows_of(place):
        return pl.ds(pl.multiple_of(place * TOK, TOK), TOK)

    def columns_of(place):
        return pl.ds(pl.multiple_of(place * HD, HD), HD)

    def own_chip(s):
        return chip_at(s, 0, 0)

    def pieces(s, target_place, source_place):
        cols = columns_of(4 * s + target_place)
        rows = rows_of(source_place)
        return (
            (keys.at[0, :, cols], kv.at[s, own_chip(s), core, 0, rows, :]),
            (values.at[0, :, cols], v_in.at[s, rows, :]),
            (queries.at[:, :, cols], q_in.at[s, :, rows, :]),
            (keys.at[1, :, cols], kv1.at[s, 0, 0, rows, :]),
            (values.at[1, :, cols], v1_in.at[s, 0, rows, :]),
        )

    def far_pieces(s, target_place, source_place):
        cols = columns_of(4 * s + target_place)
        rows = rows_of(source_place)
        return (
            (keys.at[1, :, cols], kv1.at[s, 1, 0, rows, :]),
            (values.at[1, :, cols], v1_in.at[s, 1, rows, :]),
        )

    mine = []
    for group in ((0, 1), (2,), (3, 4)):
        for step in (1, 3, 2):
            for s in range(SLOTS):
                axis = SPREAD[s]
                place = shifted(axis, step)
                both = pieces(s, place, at[axis])
                for n in group:
                    sent.append(remote(
                        *both[n], ex_send.at[s, step, n], ex_recv.at[s, step, n], device(**{axis: place})
                    ))
        for s in range(SLOTS):
            both = pieces(s, at[SPREAD[s]], at[SPREAD[s]])
            for n in group:
                copy = pltpu.make_async_copy(*both[n], local.at[s * 5 + n])
                copy.start()
                mine.append((n, copy))
    for step in range(RING):
        for s in (1, 2):
            axis = SPREAD[s]
            place = shifted(axis, step)
            both = far_pieces(s, place, at[axis])
            for n in range(2):
                sent.append(remote(
                    *both[n], ex_send.at[s, step, 5 + n], ex_recv.at[s, step, 5 + n],
                    device(y=far_y, **{axis: place}),
                ))

    fetched = []
    for n, (src, dst) in enumerate(((weight, w_buf), (hidden, h_buf), (gates, g_buf))):
        copy = pltpu.make_async_copy(src, dst, local.at[15 + n])
        copy.start()
        fetched.append(copy)

    top[...] = jnp.full(top.shape, LOWEST, jnp.float32)
    total[...] = jnp.zeros(total.shape, jnp.float32)
    acc[...] = jnp.zeros(acc.shape, jnp.float32)

    def exchanged(s, n):
        for step in (1, 3, 2):
            source = shifted(SPREAD[s], RING - step)
            src, dst = pieces(s, at[SPREAD[s]], source)[n]
            remote(src, dst, ex_send.at[s, step, n], ex_recv.at[s, step, n], sibling, start=False).wait_recv()

    def far_exchanged(s, n):
        for step in range(RING):
            source = shifted(SPREAD[s], RING - step)
            src, dst = far_pieces(s, at[SPREAD[s]], source)[n]
            remote(
                src, dst, ex_send.at[s, step, 5 + n], ex_recv.at[s, step, 5 + n], sibling, start=False
            ).wait_recv()

    def blocks_transposed(block):
        return jnp.concatenate([block[n * HD:(n + 1) * HD].T for n in range(CHUNK // HD)], axis=0)

    def chunk(s, first, second, half=None):
        where = kv.at[s, chip_routed(s, first, second), core]
        return where if half is None else where.at[half]

    slot_sends = [0] * SLOTS

    def pass_on(s, first, second, which, step, half=None):
        there = (first - step, second) if which == 0 else (first, second - step)
        there = (there[0] % RING, there[1] % RING)
        ref = chunk(s, first, second, half)
        n = slot_sends[s]
        slot_sends[s] += 1
        remote(
            ref, ref, ag_send.at[s, n],
            ag_recv.at[s, there[0], there[1], 0 if half is None else half],
            routed(s, which, step),
        )
        gathered.append((s, n, first, second, half))

    def to_sibling(s, first, second):
        ref = chunk(s, first, second)
        n = slot_sends[s]
        slot_sends[s] += 1
        place = pick(first * RING + second, second * RING + first)
        remote(ref, ref, ag_send.at[s, n], sib_recv.at[s, place], sibling)
        gathered.append((s, n, first, second, None))

    def arrive(s, first, second):
        across = first if second == 0 else second
        for half in (0, 1) if across == 2 else (None,):
            ref = chunk(s, first, second, half)
            remote(
                ref, ref, ag_send.at[s, 0],
                ag_recv.at[s, first, second, 0 if half is None else half], sibling, start=False,
            ).wait_recv()
        if second == 0:
            if first == 3:
                pass_on(s, first, second, 0, 1, 0)
            elif first == 1:
                pass_on(s, first, second, 0, 3, 1)
            pass_on(s, first, second, 1, 1)
            pass_on(s, first, second, 1, 3)
        elif second == 3:
            pass_on(s, first, second, 1, 1, 0)
        elif second == 1:
            pass_on(s, first, second, 1, 3, 1)
        to_sibling(s, first, second)

    def other_half(s, da, db):
        ref = kv.at[s, chip_at(s, da, db), 1 - core]
        remote(
            ref, ref, ag_send.at[s, 0], sib_recv.at[s, da * RING + db], sibling, start=False
        ).wait_recv()

    def masked(s, first_column, width):
        row = block_of(lax.broadcasted_iota(jnp.int32, (CHUNK, width), 0))
        column = lax.broadcasted_iota(jnp.int32, (CHUNK, width), 1) + (first_column - CHUNK)
        block = block_of(column)
        if s == 0:
            same = lax.rem(row, 2) == lax.rem(block, 2)
        else:
            same = row == block
        return same & (column >= 0)

    def soften(s, cols, scores):
        old = top[s, :, cols]
        new = jnp.maximum(old, jnp.max(scores, axis=0, keepdims=True))
        top[s, :, cols] = new
        fade = jnp.exp2((old - new) * LOG2_SCALE)
        lifted = jnp.exp2((scores - new) * LOG2_SCALE)
        total[s, :, cols] = total[s, :, cols] * fade + jnp.sum(lifted, axis=0, keepdims=True)
        return lifted.astype(jnp.bfloat16), fade

    def weigh(s, cols, value_block, lifted, fade):
        acc[s, :, cols] = acc[s, :, cols] * fade + jnp.dot(
            value_block, lifted, preferred_element_type=jnp.float32
        )

    def visit(chips, masked_slots):
        work = [(s, t) for s in range(SLOTS) for t in range(QUERIES // TILE)]
        scores, lifted = {}, {}
        for j in range(len(work) + 2):
            if j >= 2:
                s, t = work[j - 2]
                cols = slice(t * TILE, (t + 1) * TILE)
                value_block = jnp.concatenate(
                    [
                        kv[s, chips[s], half, 1, n * HD:(n + 1) * HD, :]
                        for half in (core, 1 - core)
                        for n in range(CHUNK // HD)
                    ],
                    axis=1,
                )
                weigh(s, cols, value_block, *lifted.pop(j - 2))
            if j < len(work):
                s, t = work[j]
                cols = slice(t * TILE, (t + 1) * TILE)
                key_block = jnp.concatenate(
                    [kv[s, chips[s], half, 0] for half in (core, 1 - core)], axis=0
                )
                scores[j] = jnp.dot(key_block, qt[s, :, cols], preferred_element_type=jnp.float32)
            if 1 <= j <= len(work):
                s, t = work[j - 1]
                cols = slice(t * TILE, (t + 1) * TILE)
                block = scores.pop(j - 1)
                if s in masked_slots and (t + 1) * TILE > CHUNK:
                    hide = masked(s, t * TILE, TILE)
                    block = jnp.concatenate(
                        [jnp.where(hide, LOWEST, block[:CHUNK]), block[CHUNK:]], axis=0
                    )
                lifted[j - 1] = soften(s, cols, block)

    def visit_replaced(s, w):
        cols = slice(CHUNK, QUERIES)
        block = jnp.dot(kv1[s, w, 0], qt[s, :, cols], preferred_element_type=jnp.float32)
        block = jnp.where(masked(s, CHUNK, CHUNK), block, LOWEST)
        value_block = jnp.concatenate(
            [kv1[s, w, 1, n * HD:(n + 1) * HD, :] for n in range(CHUNK // HD)], axis=1
        )
        weigh(s, cols, value_block, *soften(s, cols, block))

    for n, copy in mine:
        if n < 2:
            copy.wait()
    for s in range(SLOTS):
        exchanged(s, 0)
        exchanged(s, 1)
        kv[s, own_chip(s), core, 1] = blocks_transposed(v_in[s])
        to_sibling(s, 0, 0)
        for step in (1, 3):
            pass_on(s, 0, 0, 0, step)
            pass_on(s, 0, 0, 1, step)

    for n, copy in mine:
        if n >= 2:
            copy.wait()
    for s in range(SLOTS):
        exchanged(s, 2)
        for step in range(2):
            for n in range(CHUNK // HD):
                start = step * CHUNK + n * HD
                qt[s, :, start:start + HD] = q_in[s, step, n * HD:(n + 1) * HD, :].T
    for s in range(SLOTS):
        other_half(s, 0, 0)
    visit([own_chip(s) for s in range(SLOTS)], (0, 1, 2))
    for s in range(SLOTS):
        for w in (0,) if s == 0 else (0, 1):
            for n in range(2):
                if w == 0:
                    exchanged(s, 3 + n)
                else:
                    far_exchanged(s, n)
            kv1[s, w, 1] = blocks_transposed(v1_in[s, w])
            visit_replaced(s, w)

    def turn(r, carry):
        for at_visit, arrivals in ARRIVALS.items():
            @pl.when(r == at_visit)
            def _():
                for place in arrivals:
                    for s in range(SLOTS):
                        arrive(s, *place)

        da = sum((r == n).astype(jnp.int32) * place[0] for n, place in enumerate(VISITS))
        db = sum((r == n).astype(jnp.int32) * place[1] for n, place in enumerate(VISITS))
        for s in range(SLOTS):
            other_half(s, da, db)
        visit([chip_at(s, da, db) for s in range(SLOTS)], ())
        return carry

    lax.fori_loop(0, len(VISITS), turn, 0)

    for s in range(SLOTS):
        other_half(s, *PARTNER)
    visit([chip_at(s, *PARTNER) for s in range(SLOTS)], (1, 2))

    returns = []
    for s in range(SLOTS):
        axis = SPREAD[s]
        result = (acc[s] / total[s]).astype(jnp.bfloat16)
        for step in range(2):
            o_out[s, step] = jnp.concatenate(
                [
                    result[:, step * CHUNK + n * HD:step * CHUNK + (n + 1) * HD].T
                    for n in range(CHUNK // HD)
                ],
                axis=0,
            )
        cols = columns_of(4 * s + at[axis])
        for step in (2, 1, 3):
            place = shifted(axis, step)
            sent.append(remote(
                o_out.at[s, :, rows_of(place), :], att.at[:, :, cols],
                ret_send.at[s, step], ret_recv.at[s, step], device(**{axis: place}),
            ))
        copy = pltpu.make_async_copy(o_out.at[s, :, rows_of(at[axis]), :], att.at[:, :, cols], local.at[18 + s])
        copy.start()
        returns.append(copy)
    for copy in fetched + returns:
        copy.wait()
    for s in range(SLOTS):
        axis = SPREAD[s]
        for step in (1, 3, 2):
            source = shifted(axis, RING - step)
            remote(
                o_out.at[s, :, rows_of(at[axis]), :], att.at[:, :, columns_of(4 * s + source)],
                ret_send.at[s, step], ret_recv.at[s, step], sibling, start=False,
            ).wait_recv()

    merged = att[...].reshape(2 * TOK, att.shape[2])
    width = out.shape[2]
    for n in range(0, width, 512):
        cols = slice(n, n + 512)
        projected = jnp.dot(merged, w_buf[:, cols], preferred_element_type=jnp.float32)
        for step in range(2):
            gate = g_buf[pl.ds(steps[step], 1), cols]
            block = projected[step * TOK:(step + 1) * TOK]
            out[step, :, cols] = (h_buf[step, :, cols].astype(jnp.float32) + gate * block).astype(out.dtype)

    for copy in sent:
        copy.wait_send()
    for s, n, first, second, half in gathered:
        ref = chunk(s, first, second, half)
        remote(ref, ref, ag_send.at[s, n], ag_recv.at[s, 0, 0, 0], sibling, start=False).wait_send()


def shards(hidden, queries, keys, values, out_weight, gate_table, steps_t):
    any_spec = pl.BlockSpec(memory_space=pl.ANY)
    dma = pltpu.SemaphoreType.DMA
    bf16, f32 = jnp.bfloat16, jnp.float32
    return pl.pallas_call(
        kernel,
        out_shape=jax.ShapeDtypeStruct(hidden.shape, hidden.dtype),
        in_specs=[any_spec] * 6 + [pl.BlockSpec(memory_space=pltpu.SMEM)],
        out_specs=pl.BlockSpec(memory_space=pltpu.VMEM),
        scratch_shapes=[
            pltpu.VMEM((SLOTS, RING * RING, 2, 2, CHUNK, HD), bf16),
            pltpu.VMEM((SLOTS, 2, 2, CHUNK, HD), bf16),
            pltpu.VMEM((SLOTS, CHUNK, HD), bf16),
            pltpu.VMEM((SLOTS, 2, CHUNK, HD), bf16),
            pltpu.VMEM((SLOTS, 2, CHUNK, HD), bf16),
            pltpu.VMEM((SLOTS, HD, QUERIES), bf16),
            pltpu.VMEM((SLOTS, HD, QUERIES), f32),
            pltpu.VMEM((SLOTS, 1, QUERIES), f32),
            pltpu.VMEM((SLOTS, 1, QUERIES), f32),
            pltpu.VMEM((SLOTS, 2, CHUNK, HD), bf16),
            pltpu.VMEM(queries.shape, bf16),
            pltpu.VMEM(out_weight.shape, bf16),
            pltpu.VMEM(gate_table.shape, f32),
            pltpu.VMEM(hidden.shape, bf16),
            dma((SLOTS, RING, 7)),
            dma((SLOTS, RING, 7)),
            dma((SLOTS, 36)),
            dma((SLOTS, RING, RING, 2)),
            dma((SLOTS, RING * RING)),
            dma((SLOTS, RING)),
            dma((SLOTS, RING)),
            dma((21,)),
        ],
        compiler_params=pltpu.CompilerParams(
            collective_id=0, has_side_effects=True, vmem_limit_bytes=58 * 2**20
        ),
        name="attend",
    )(hidden, queries, keys, values, out_weight, gate_table, steps_t)


def solution(mesh):
    rows = P(None, ("patch", "head"), None)
    return jax.shard_map(
        shards,
        mesh=mesh,
        in_specs=(rows, rows, rows, rows, P(), P(), P()),
        out_specs=rows,
        check_vma=False,
    )
```

time: 577 us -> 104 us (0.18)
  waiting for transfers between devices: 238 us -> 0 us
  local copies, waits for them, and re-layouts: 165 us -> 2.36 us
  Pallas kernels: 0 us -> 101 us
  matrix products: 87.8 us -> 0 us
  other arithmetic: 25.6 us -> 0 us
  starting transfers between devices: 22.5 us -> 0 us
  blocking collectives: 19.8 us -> 0 us
  between operations: 13.7 us -> 0.01 us
    all_gather x2 -> x0, waiting for transfers between devices: 224 us -> none  [the longest x1 127 us: shards(): lax.all_gather(first_v, 'patch', axis=0, tiled=True)]
    dynamic_slice x48 -> x0, local copies, waits for them, and re-layouts: 149 us -> none  [the longest x32 110 us: visit(): value_block = lax.dynamic_slice_in_dim(value_table, offset, block_rows, 0)]
    pallas_call x0 -> x1, Pallas kernels: none -> 101 us  [shards(): pl.pallas_call(kernel, out_shape=jax.ShapeDtypeStruct(hidden.shape, hidde...]
    dot_general x34 -> x0, matrix products: 87.8 us -> none  [the longest x16 46 us: absorb(): jnp.einsum('qhd,khd->hqk', query_heads, key_heads, preferred_element_type...]
    all_to_all x6 -> x0, starting transfers between devices: 22.5 us -> none  [the longest x2 7.66 us: finish(): lax.all_to_all(attended, 'head', split_axis=0, concat_axis=1, tiled=True)]
    reduce_sum x17 -> x0, other arithmetic: 22.3 us -> none  [the longest x16 21.1 us: absorb(): weight_sum = weight_sum * rescale + jnp.sum(lifted, axis=-1)]
    all_to_all x2 -> x0, blocking collectives: 19.8 us -> none  [the longest x1 11 us: regroup(): lax.all_to_all(key_split, 'head', split_axis=1, concat_axis=0, tiled=True)]
    all_to_all x6 -> x0, waiting for transfers between devices: 14 us -> none  [the longest x2 6.46 us: regroup(): lax.all_to_all(query_split, 'head', split_axis=1, concat_axis=0, tiled=True)]
  transfers between devices with their start and end apart: 8 -> 0, of which waited for: 6 -> 0; matrix products, arithmetic and copies ran while one was open for 46% -> 0% of each run, Pallas kernels for 0% -> 0%
where the time goes in v1:
time: 104 us
  Pallas kernels  101 us (97%)
  local copies, waits for them, and re-layouts  2.36 us (2%)
    pallas_call x1, Pallas kernels, shards(): pl.pallas_call(kernel, out_shape=jax.ShapeDtypeStruct(hidden.shape, hidde...  101 us
    unnamed x1, local copies, waits for them, and re-layouts  2.36 us

profile of v1, /device:TPU:1, one launch (start us, length us, event | category | flops | bytes accessed | tf_op | source)
XLA Modules:
  0.0 103.8 jit_solution(8837347277349253741)
XLA Ops:
  0.0 101.4 %attend.1 = bf16[2,96,3072]{2,1,0:T(8,128)(2,1)} custom-call(bf16[2,96,3072]{2,1,0:T(8,128)(2,1)} %hidden.1, bf16[2,96,1536]{2,1,0:T(8,128)(2,1)} %queries.1, bf16[2,96,1536]{2,1,0:T(8,128)(2,1)} %keys.1, bf16[2,96,1536]{2,1,0:T(8,128)(2,1)} %values.1, bf16[1536,3072]{1,0:T(8,128)(2,1)} %weight.1, f32[50,3072]{1,0:T(8,128)} %gates.1, s32[2]{0:T(128)} %steps.1), custom_call_target="tpu_custom_call" | custom-call | tf_op jit(solution)/shard_map/attend/pallas_call | solution.py:418
  101.4 2.4 %copy.9 = bf16[2,96,3072]{2,1,0:T(8,128)(2,1)} copy(bf16[2,96,3072]{2,1,0:T(8,128)(2,1)} %attend.1) | data formatting | bytes 2359296

commit v2 on v1

v2 whole, which is shorter than its diff:
```python
import functools
import math

import jax
import jax.numpy as jnp
from jax import lax
from jax.experimental import pallas as pl
from jax.experimental.pallas import tpu as pltpu
from jax.sharding import PartitionSpec as P

HD = 128
TOK = 96
CHUNK = 4 * TOK
QUERIES = 2 * CHUNK
RING = 4
SLOTS = 3
TILE = 256
LOG2_SCALE = math.log2(math.e) / math.sqrt(HD)
LOWEST = -1e30
SUMS = 16

SPREAD = ("y", "x", "z")
PLANE = (("x", "z"), ("y", "z"), ("y", "x"))

VISITS = (
    ((1, 0), (3, 0)), ((0, 1), (0, 3)), ((1, 1), (1, 3)), ((3, 1), (3, 3)),
    ((2, 1), (2, 3)), (None, (1, 2)), ((3, 2), (2, 2)),
)
FREE = (0, 2)
PARTNER = (2, 0)

ARRIVALS = {
    0: ((1, 0), (3, 0)),
    2: ((0, 1), (0, 3)),
    3: ((2, 0),),
    4: ((1, 1), (1, 3)),
    6: ((3, 1), (3, 3)),
    8: ((2, 1), (2, 3), (0, 2)),
    10: ((1, 2),),
    12: ((3, 2), (2, 2)),
}
PASSES = {
    0: (
        ((0, 0), 1, 1, None), ((0, 0), 1, 3, None),
        ((3, 0), 0, 1, 0), ((1, 0), 0, 3, 1),
    ),
    1: (((1, 0), 1, 1, None), ((1, 0), 1, 3, None)),
    3: (((3, 0), 1, 1, None), ((3, 0), 1, 3, None)),
    4: (((0, 3), 1, 1, 0), ((0, 1), 1, 3, 1)),
    5: (((2, 0), 1, 1, None), ((2, 0), 1, 3, None)),
    6: (((1, 3), 1, 1, 0), ((1, 1), 1, 3, 1)),
    7: (((3, 3), 1, 1, 0), ((3, 1), 1, 3, 1)),
    8: (((2, 3), 1, 1, 0), ((2, 1), 1, 3, 1)),
}
HAND_ON = 6


def block_of(index):
    return sum((index >= edge * TOK).astype(jnp.int32) for edge in range(1, RING))


def kernel(
    hidden, queries, keys, values, weight, gates, steps, out,
    kv, kv1, v_in, v1_in, q_in, qt, acc, top, part, level, o_out, att, w_buf, g_buf, h_buf,
    ex_send, ex_recv, ag_send, ag_recv, sib_send, sib_recv, far_send, far_recv, ret_send, ret_recv, local,
):
    patch, head = lax.axis_index("patch"), lax.axis_index("head")
    core = lax.rem(patch, 2)
    at = {
        "x": patch // 16,
        "z": lax.rem(patch // 4, RING),
        "y": head * 2 + lax.rem(patch // 2, 2),
    }

    def device(**moved):
        pos = dict(at, core=core)
        pos.update(moved)
        y = pos["y"]
        return (((pos["x"] * RING + pos["z"]) * 2 + lax.rem(y, 2)) * 2 + pos["core"], y // 2)

    def shifted(axis, step):
        return lax.rem(at[axis] + step, RING)

    def pick(first, second):
        return first + core * (second - first)

    def routed(s, which, step):
        a, b = PLANE[s] if which == 0 else PLANE[s][::-1]
        da, db = device(**{a: shifted(a, step)}), device(**{b: shifted(b, step)})
        return (pick(da[0], db[0]), pick(da[1], db[1]))

    def chip_at(s, da, db):
        a, b = PLANE[s]
        return shifted(a, da) * RING + shifted(b, db)

    def chip_routed(s, first, second):
        return pick(chip_at(s, first, second), chip_at(s, second, first))

    sibling = device(core=1 - core)
    far_y = shifted("y", 2)

    peers = [device(**{axis: shifted(axis, step)}) for axis in "xyz" for step in (1, 2, 3)]
    peers.append(sibling)
    barrier = pltpu.get_barrier_semaphore()
    for peer in peers:
        pl.semaphore_signal(barrier, inc=1, device_id=peer, device_id_type=pl.DeviceIdType.MESH)

    sent, gathered = [], []

    def remote(src, dst, send_sem, recv_sem, target, start=True):
        copy = pltpu.make_async_remote_copy(
            src_ref=src, dst_ref=dst, send_sem=send_sem, recv_sem=recv_sem,
            device_id=target, device_id_type=pl.DeviceIdType.MESH,
        )
        if start:
            copy.start()
        return copy

    def rows_of(place):
        return pl.ds(pl.multiple_of(place * TOK, TOK), TOK)

    def columns_of(place):
        return pl.ds(pl.multiple_of(place * HD, HD), HD)

    def own_chip(s):
        return chip_at(s, 0, 0)

    def pieces(s, target_place, source_place):
        cols = columns_of(4 * s + target_place)
        rows = rows_of(source_place)
        return (
            (keys.at[0, :, cols], kv.at[s, own_chip(s), 0, rows, :]),
            (values.at[0, :, cols], v_in.at[s, rows, :]),
            (queries.at[:, :, cols], q_in.at[0, s, :, rows, :]),
            (keys.at[1, :, cols], kv1.at[s, 0, 0, rows, :]),
            (values.at[1, :, cols], v1_in.at[s, rows, :]),
        )

    def exchange(group):
        for step in (1, 3, 2):
            for s in range(SLOTS):
                axis = SPREAD[s]
                place = shifted(axis, step)
                both = pieces(s, place, at[axis])
                for n in group:
                    sent.append(remote(
                        *both[n], ex_send.at[s, step, n], ex_recv.at[s, step, n], device(**{axis: place})
                    ))

    mine = []
    for n in range(5):
        for s in range(SLOTS):
            copy = pltpu.make_async_copy(*pieces(s, at[SPREAD[s]], at[SPREAD[s]])[n], local.at[s * 5 + n])
            copy.start()
            mine.append((n, copy))
    fetched = []
    for n, (src, dst) in enumerate(((weight, w_buf), (hidden, h_buf), (gates, g_buf))):
        copy = pltpu.make_async_copy(src, dst, local.at[15 + n])
        copy.start()
        fetched.append(copy)

    top[...] = jnp.full(top.shape, LOWEST, jnp.float32)
    acc[...] = jnp.zeros(acc.shape, jnp.float32)

    pl.semaphore_wait(barrier, len(peers))
    exchange((0, 1))
    exchange((2,))

    def exchanged(s, n):
        for step in (1, 3, 2):
            source = shifted(SPREAD[s], RING - step)
            src, dst = pieces(s, at[SPREAD[s]], source)[n]
            remote(src, dst, ex_send.at[s, step, n], ex_recv.at[s, step, n], sibling, start=False).wait_recv()

    def blocks_transposed(block):
        return jnp.concatenate([block[n * HD:(n + 1) * HD].T for n in range(CHUNK // HD)], axis=0)

    def chunk(s, first, second, half=None):
        where = kv.at[s, chip_routed(s, first, second)]
        return where if half is None else where.at[half]

    slot_sends = [0] * SLOTS

    def pass_on(s, first, second, which, step, half=None):
        there = (first - step, second) if which == 0 else (first, second - step)
        there = (there[0] % RING, there[1] % RING)
        ref = chunk(s, first, second, half)
        n = slot_sends[s]
        slot_sends[s] += 1
        remote(
            ref, ref, ag_send.at[s, n],
            ag_recv.at[s, there[0], there[1], 0 if half is None else half],
            routed(s, which, step),
        )
        gathered.append((s, n, first, second, half))

    def arrive(s, first, second):
        across = first if second == 0 else second
        for half in (0, 1) if across == 2 else (None,):
            ref = chunk(s, first, second, half)
            remote(
                ref, ref, ag_send.at[s, 0],
                ag_recv.at[s, first, second, 0 if half is None else half], sibling, start=False,
            ).wait_recv()

    def to_sibling(n, src, dst):
        return remote(src, dst, sib_send.at[n], sib_recv.at[n], sibling, start=False)

    def sibling_queries(s):
        return to_sibling(s, q_in.at[0, s], q_in.at[1, s])

    def partial(s):
        return (
            to_sibling(3 + 2 * s, part.at[0, s], part.at[1, s]),
            to_sibling(4 + 2 * s, level.at[0, s], level.at[1, s]),
        )

    def masked(s, first_column, width):
        row = block_of(lax.broadcasted_iota(jnp.int32, (CHUNK, width), 0))
        column = lax.broadcasted_iota(jnp.int32, (CHUNK, width), 1) + (first_column - CHUNK)
        block = block_of(column)
        if s == 0:
            same = lax.rem(row, 2) == lax.rem(block, 2)
        else:
            same = row == block
        return same & (column >= 0)

    def soften(q, s, cols, scores):
        old = top[q, s, :, cols]
        new = jnp.maximum(old, jnp.max(scores, axis=0, keepdims=True))
        top[q, s, :, cols] = new
        return jnp.exp2(scores - new).astype(jnp.bfloat16), jnp.exp2(old - new)

    def score(q, s, cols, key_block):
        return jnp.dot(
            jnp.concatenate([key_block, key_block], axis=1), qt[q, s, :, cols],
            preferred_element_type=jnp.float32,
        )

    def weigh(q, s, cols, value_blocks, lifted, fade):
        value_block = jnp.concatenate(value_blocks, axis=1)
        ones = jnp.ones((SUMS, value_block.shape[1]), value_block.dtype)
        acc[q, s, :, cols] = acc[q, s, :, cols] * fade + jnp.dot(
            jnp.concatenate([value_block, ones], axis=0), lifted, preferred_element_type=jnp.float32
        )

    def visit(q, chips, masked_slots):
        work = [(s, slice(t, t + TILE)) for s in range(SLOTS) for t in range(0, QUERIES, TILE)]
        scores, lifted = {}, {}
        for j in range(len(work) + 2):
            if j >= 2:
                s, cols = work[j - 2]
                value_blocks = [
                    kv[s, chip, 1, n * HD:(n + 1) * HD, :] for chip in chips[s] for n in range(CHUNK // HD)
                ]
                weigh(q, s, cols, value_blocks, *lifted.pop(j - 2))
            if j < len(work):
                s, cols = work[j]
                key_block = jnp.concatenate([kv[s, chip, 0] for chip in chips[s]], axis=0)
                scores[j] = score(q, s, cols, key_block)
            if 1 <= j <= len(work):
                s, cols = work[j - 1]
                block = scores.pop(j - 1)
                if s in masked_slots and cols.stop > CHUNK:
                    block = jnp.where(masked(s, cols.start, TILE), LOWEST, block)
                lifted[j - 1] = soften(q, s, cols, block)

    def visit_replaced(s, w):
        cols = slice(CHUNK, QUERIES)
        block = score(0, s, cols, kv1[s, w, 0])
        block = jnp.where(masked(s, CHUNK, CHUNK), block, LOWEST)
        value_blocks = [kv1[s, w, 1, n * HD:(n + 1) * HD, :] for n in range(CHUNK // HD)]
        weigh(0, s, cols, value_blocks, *soften(0, s, cols, block))

    def turn_queries(q):
        for s in range(SLOTS):
            for step in range(2):
                for n in range(CHUNK // HD):
                    start = step * CHUNK + n * HD
                    scaled = q_in[q, s, step, n * HD:(n + 1) * HD, :].astype(jnp.float32).T * LOG2_SCALE
                    high = scaled.astype(jnp.bfloat16)
                    qt[q, s, :HD, start:start + HD] = high
                    qt[q, s, HD:, start:start + HD] = (scaled - high.astype(jnp.float32)).astype(jnp.bfloat16)

    for n, copy in mine:
        if n < 2:
            copy.wait()
    for s in range(SLOTS):
        exchanged(s, 0)
        exchanged(s, 1)
        kv[s, own_chip(s), 1] = blocks_transposed(v_in[s])
        for step in (1, 3):
            pass_on(s, 0, 0, 0, step)

    for n, copy in mine:
        if n >= 2:
            copy.wait()
    for s in range(SLOTS):
        exchanged(s, 2)
        sibling_queries(s).start()
    exchange((3, 4))
    turn_queries(0)
    own = [(own_chip(s),) for s in range(SLOTS)]
    visit(0, own, (0, 1, 2))
    for s in range(SLOTS):
        sibling_queries(s).wait_recv()
    turn_queries(1)
    visit(1, own, ())

    def replacement(s):
        ref = kv1.at[s, 0]
        return remote(
            ref, kv1.at[s, 1], far_send.at[s], far_recv.at[s], device(y=far_y), start=False
        )

    def hand_on():
        for s in range(SLOTS):
            exchanged(s, 3)
            exchanged(s, 4)
            kv1[s, 0, 1] = blocks_transposed(v1_in[s])
            if s > 0:
                replacement(s).start()

    def turn(r, carry):
        for k in range(2 * len(VISITS)):
            if k in ARRIVALS or k in PASSES:
                @pl.when(r == k)
                def _():
                    for s in range(SLOTS):
                        for place in ARRIVALS.get(k, ()):
                            arrive(s, *place)
                    for place, which, step, half in PASSES.get(k, ()):
                        for s in range(SLOTS):
                            pass_on(s, *place, which, step, half)

        pl.when(r == HAND_ON)(hand_on)
        pair = r // 2
        chips = []
        for s in range(SLOTS):
            places = [
                [
                    chip_at(s, *FREE) if place is None else chip_routed(s, *place)
                    for place in (visited[side] for visited in VISITS)
                ]
                for side in range(2)
            ]
            chips.append([
                sum((pair == n).astype(jnp.int32) * place for n, place in enumerate(places[side]))
                for side in range(2)
            ])
        visit(lax.rem(r, 2), chips, ())
        return carry

    lax.fori_loop(0, 2 * len(VISITS), turn, 0)

    partner = [(chip_at(s, *PARTNER),) for s in range(SLOTS)]
    visit(1, partner, ())
    for s in range(SLOTS):
        weight_sum = acc[1, s, HD:HD + 1]
        part[0, s] = (acc[1, s, :HD] / weight_sum).astype(jnp.bfloat16)
        level[0, s] = jnp.broadcast_to(top[1, s] + jnp.log2(weight_sum), level.shape[2:])
        for copy in partial(s):
            copy.start()
    visit(0, partner, (1, 2))
    for s in range(SLOTS):
        visit_replaced(s, 0)
        if s > 0:
            replacement(s).wait_recv()
            visit_replaced(s, 1)

    returns = []
    for s in range(SLOTS):
        axis = SPREAD[s]
        for copy in partial(s):
            copy.wait_recv()
        weight_sum = acc[0, s, HD:HD + 1]
        gap = level[1, s, 0:1] - (top[0, s] + jnp.log2(weight_sum))
        result = (
            acc[0, s, :HD] / (weight_sum * (1.0 + jnp.exp2(gap)))
            + part[1, s].astype(jnp.float32) / (1.0 + jnp.exp2(-gap))
        ).astype(jnp.bfloat16)
        for step in range(2):
            o_out[s, step] = jnp.concatenate(
                [
                    result[:, step * CHUNK + n * HD:step * CHUNK + (n + 1) * HD].T
                    for n in range(CHUNK // HD)
                ],
                axis=0,
            )
        cols = columns_of(4 * s + at[axis])
        for step in (2, 1, 3):
            place = shifted(axis, step)
            sent.append(remote(
                o_out.at[s, :, rows_of(place), :], att.at[:, :, cols],
                ret_send.at[s, step], ret_recv.at[s, step], device(**{axis: place}),
            ))
        copy = pltpu.make_async_copy(o_out.at[s, :, rows_of(at[axis]), :], att.at[:, :, cols], local.at[18 + s])
        copy.start()
        returns.append(copy)
    for copy in fetched + returns:
        copy.wait()
    for s in range(SLOTS):
        axis = SPREAD[s]
        for step in (1, 3, 2):
            source = shifted(axis, RING - step)
            remote(
                o_out.at[s, :, rows_of(at[axis]), :], att.at[:, :, columns_of(4 * s + source)],
                ret_send.at[s, step], ret_recv.at[s, step], sibling, start=False,
            ).wait_recv()

    merged = att[...].reshape(2 * TOK, att.shape[2])
    width = out.shape[2]
    for n in range(0, width, 512):
        cols = slice(n, n + 512)
        projected = jnp.dot(merged, w_buf[:, cols], preferred_element_type=jnp.float32)
        for step in range(2):
            gate = g_buf[pl.ds(steps[step], 1), cols]
            block = projected[step * TOK:(step + 1) * TOK]
            out[step, :, cols] = (h_buf[step, :, cols].astype(jnp.float32) + gate * block).astype(out.dtype)

    for copy in sent:
        copy.wait_send()
    for s in (1, 2):
        replacement(s).wait_send()
    for s in range(SLOTS):
        for copy in (sibling_queries(s),) + partial(s):
            copy.wait_send()
    for s, n, first, second, half in gathered:
        ref = chunk(s, first, second, half)
        remote(ref, ref, ag_send.at[s, n], ag_recv.at[s, 0, 0, 0], sibling, start=False).wait_send()


def shards(hidden, queries, keys, values, out_weight, gate_table, steps_t):
    any_spec = pl.BlockSpec(memory_space=pl.ANY)
    dma = pltpu.SemaphoreType.DMA
    bf16, f32 = jnp.bfloat16, jnp.float32
    return pl.pallas_call(
        kernel,
        out_shape=jax.ShapeDtypeStruct(hidden.shape, hidden.dtype),
        in_specs=[any_spec] * 6 + [pl.BlockSpec(memory_space=pltpu.SMEM)],
        out_specs=pl.BlockSpec(memory_space=pltpu.VMEM),
        scratch_shapes=[
            pltpu.VMEM((SLOTS, RING * RING, 2, CHUNK, HD), bf16),
            pltpu.VMEM((SLOTS, 2, 2, CHUNK, HD), bf16),
            pltpu.VMEM((SLOTS, CHUNK, HD), bf16),
            pltpu.VMEM((SLOTS, CHUNK, HD), bf16),
            pltpu.VMEM((2, SLOTS, 2, CHUNK, HD), bf16),
            pltpu.VMEM((2, SLOTS, 2 * HD, QUERIES), bf16),
            pltpu.VMEM((2, SLOTS, HD + SUMS, QUERIES), f32),
            pltpu.VMEM((2, SLOTS, 1, QUERIES), f32),
            pltpu.VMEM((2, SLOTS, HD, QUERIES), bf16),
            pltpu.VMEM((2, SLOTS, 8, QUERIES), f32),
            pltpu.VMEM((SLOTS, 2, CHUNK, HD), bf16),
            pltpu.VMEM(queries.shape, bf16),
            pltpu.VMEM(out_weight.shape, bf16),
            pltpu.VMEM(gate_table.shape, f32),
            pltpu.VMEM(hidden.shape, bf16),
            dma((SLOTS, RING, 5)),
            dma((SLOTS, RING, 5)),
            dma((SLOTS, 20)),
            dma((SLOTS, RING, RING, 2)),
            dma((9,)),
            dma((9,)),
            dma((SLOTS,)),
            dma((SLOTS,)),
            dma((SLOTS, RING)),
            dma((SLOTS, RING)),
            dma((21,)),
        ],
        compiler_params=pltpu.CompilerParams(
            collective_id=0, has_side_effects=True, vmem_limit_bytes=58 * 2**20
        ),
        name="attend",
    )(hidden, queries, keys, values, out_weight, gate_table, steps_t)


def solution(mesh):
    rows = P(None, ("patch", "head"), None)
    return jax.shard_map(
        shards,
        mesh=mesh,
        in_specs=(rows, rows, rows, rows, P(), P(), P()),
        out_specs=rows,
        check_vma=False,
    )
```

time: 104 us -> 85.7 us (0.82)
  Pallas kernels: 101 us -> 83.2 us
    pallas_call x1, Pallas kernels: 101 us -> 83.2 us  [shards(): pl.pallas_call(kernel, out_shape=jax.ShapeDtypeStruct(hidden.shape, hidde...]
where the time goes in v2:
time: 85.7 us; the launch traced here: 85.5 us
  Pallas kernels  83.2 us (97%)
  local copies, waits for them, and re-layouts  2.36 us (3%)
    pallas_call x1, Pallas kernels, shards(): pl.pallas_call(kernel, out_shape=jax.ShapeDtypeStruct(hidden.shape, hidde...  83.2 us
    unnamed x1, local copies, waits for them, and re-layouts  2.36 us

profile of v2, /device:TPU:1, one launch (start us, length us, event | category | flops | bytes accessed | tf_op | source)
XLA Modules:
  0.0 85.5 jit_solution(14529045255879447846)
XLA Ops:
  0.0 83.2 %attend.1 = bf16[2,96,3072]{2,1,0:T(8,128)(2,1)} custom-call(bf16[2,96,3072]{2,1,0:T(8,128)(2,1)} %hidden.1, bf16[2,96,1536]{2,1,0:T(8,128)(2,1)} %queries.1, bf16[2,96,1536]{2,1,0:T(8,128)(2,1)} %keys.1, bf16[2,96,1536]{2,1,0:T(8,128)(2,1)} %values.1, bf16[1536,3072]{1,0:T(8,128)(2,1)} %weight.1, f32[50,3072]{1,0:T(8,128)} %gates.1, s32[2]{0:T(128)} %steps.1), custom_call_target="tpu_custom_call" | custom-call | tf_op jit(solution)/shard_map/attend/pallas_call | solution.py:437
  83.2 2.4 %copy.9 = bf16[2,96,3072]{2,1,0:T(8,128)(2,1)} copy(bf16[2,96,3072]{2,1,0:T(8,128)(2,1)} %attend.1) | data formatting | bytes 2359296

commit v3 on v2

--- a/solution.py
+++ b/solution.py
@@ -32,11 +32,11 @@
 ARRIVALS = {
     0: ((1, 0), (3, 0)),
     2: ((0, 1), (0, 3)),
-    3: ((2, 0),),
     4: ((1, 1), (1, 3)),
+    5: ((2, 0),),
     6: ((3, 1), (3, 3)),
-    8: ((2, 1), (2, 3), (0, 2)),
-    10: ((1, 2),),
+    8: ((2, 1), (2, 3)),
+    10: ((0, 2), (1, 2)),
     12: ((3, 2), (2, 2)),
 }
 PASSES = {
@@ -52,7 +52,8 @@
     7: (((3, 3), 1, 1, 0), ((3, 1), 1, 3, 1)),
     8: (((2, 3), 1, 1, 0), ((2, 1), 1, 3, 1)),
 }
-HAND_ON = 6
+HAND_ON = 10
+WITH_PARTNER = 10
 
 
 def block_of(index):
@@ -61,7 +62,7 @@
 
 def kernel(
     hidden, queries, keys, values, weight, gates, steps, out,
-    kv, kv1, v_in, v1_in, q_in, qt, acc, top, part, level, o_out, att, w_buf, g_buf, h_buf,
+    kv, kv1, between, v_in, v1_in, q_in, qt, acc, top, part, level, o_out, att, w_buf, g_buf, h_buf,
     ex_send, ex_recv, ag_send, ag_recv, sib_send, sib_recv, far_send, far_recv, ret_send, ret_recv, local,
 ):
     patch, head = lax.axis_index("patch"), lax.axis_index("head")
@@ -97,7 +98,6 @@
         return pick(chip_at(s, first, second), chip_at(s, second, first))
 
     sibling = device(core=1 - core)
-    far_y = shifted("y", 2)
 
     peers = [device(**{axis: shifted(axis, step)}) for axis in "xyz" for step in (1, 2, 3)]
     peers.append(sibling)
@@ -307,10 +307,13 @@
     turn_queries(1)
     visit(1, own, ())
 
-    def replacement(s):
-        ref = kv1.at[s, 0]
+    def replacement(s, half, hop):
+        source = kv1.at[s, 0, half] if hop == 0 else between.at[s, half]
+        target = between.at[s, half] if hop == 0 else kv1.at[s, 1, half]
+        step = (1, 3)[half]
         return remote(
-            ref, kv1.at[s, 1], far_send.at[s], far_recv.at[s], device(y=far_y), start=False
+            source, target, far_send.at[s, half, hop], far_recv.at[s, half, hop],
+            device(y=shifted("y", step)), start=False,
         )
 
     def hand_on():
@@ -319,7 +322,29 @@
             exchanged(s, 4)
             kv1[s, 0, 1] = blocks_transposed(v1_in[s])
             if s > 0:
-                replacement(s).start()
+                for half in range(2):
+                    replacement(s, half, 0).start()
+
+    def hand_over():
+        for s in (1, 2):
+            for half in range(2):
+                replacement(s, half, 0).wait_recv()
+                replacement(s, half, 1).start()
+
+    def with_partner():
+        partner = [(chip_at(s, *PARTNER),) for s in range(SLOTS)]
+        visit(1, partner, ())
+        visit(0, partner, (1, 2))
+        for s in range(SLOTS):
+            visit_replaced(s, 0)
+
+    def sibling_done():
+        for s in range(SLOTS):
+            weight_sum = acc[1, s, HD:HD + 1]
+            part[0, s] = (acc[1, s, :HD] / weight_sum).astype(jnp.bfloat16)
+            level[0, s] = jnp.broadcast_to(top[1, s] + jnp.log2(weight_sum), level.shape[2:])
+            for copy in partial(s):
+                copy.start()
 
     def turn(r, carry):
         for k in range(2 * len(VISITS)):
@@ -334,6 +359,9 @@
                             pass_on(s, *place, which, step, half)
 
         pl.when(r == HAND_ON)(hand_on)
+        pl.when(r == HAND_ON + 2)(hand_over)
+        pl.when(r == WITH_PARTNER)(with_partner)
+        pl.when(r == 2 * len(VISITS) - 1)(sibling_done)
         pair = r // 2
         chips = []
         for s in range(SLOTS):
@@ -348,25 +376,14 @@
                 sum((pair == n).astype(jnp.int32) * place for n, place in enumerate(places[side]))
                 for side in range(2)
             ])
-        visit(lax.rem(r, 2), chips, ())
+        visit(1 - lax.rem(r, 2), chips, ())
         return carry
 
     lax.fori_loop(0, 2 * len(VISITS), turn, 0)
-
-    partner = [(chip_at(s, *PARTNER),) for s in range(SLOTS)]
-    visit(1, partner, ())
-    for s in range(SLOTS):
-        weight_sum = acc[1, s, HD:HD + 1]
-        part[0, s] = (acc[1, s, :HD] / weight_sum).astype(jnp.bfloat16)
-        level[0, s] = jnp.broadcast_to(top[1, s] + jnp.log2(weight_sum), level.shape[2:])
-        for copy in partial(s):
-            copy.start()
-    visit(0, partner, (1, 2))
-    for s in range(SLOTS):
-        visit_replaced(s, 0)
-        if s > 0:
-            replacement(s).wait_recv()
-            visit_replaced(s, 1)
+    for s in (1, 2):
+        for half in range(2):
+            replacement(s, half, 1).wait_recv()
+        visit_replaced(s, 1)
 
     returns = []
     for s in range(SLOTS):
@@ -421,7 +438,9 @@
     for copy in sent:
         copy.wait_send()
     for s in (1, 2):
-        replacement(s).wait_send()
+        for half in range(2):
+            for hop in range(2):
+                replacement(s, half, hop).wait_send()
     for s in range(SLOTS):
         for copy in (sibling_queries(s),) + partial(s):
             copy.wait_send()
@@ -442,6 +461,7 @@
         scratch_shapes=[
             pltpu.VMEM((SLOTS, RING * RING, 2, CHUNK, HD), bf16),
             pltpu.VMEM((SLOTS, 2, 2, CHUNK, HD), bf16),
+            pltpu.VMEM((SLOTS, 2, CHUNK, HD), bf16),
             pltpu.VMEM((SLOTS, CHUNK, HD), bf16),
             pltpu.VMEM((SLOTS, CHUNK, HD), bf16),
             pltpu.VMEM((2, SLOTS, 2, CHUNK, HD), bf16),
@@ -461,8 +481,8 @@
             dma((SLOTS, RING, RING, 2)),
             dma((9,)),
             dma((9,)),
-            dma((SLOTS,)),
-            dma((SLOTS,)),
+            dma((SLOTS, 2, 2)),
+            dma((SLOTS, 2, 2)),
             dma((SLOTS, RING)),
             dma((SLOTS, RING)),
             dma((21,)),

time: 85.7 us -> 84.1 us (0.981)
  Pallas kernels: 83.2 us -> 81.6 us
    pallas_call x1, Pallas kernels: 83.2 us -> 81.6 us  [shards(): pl.pallas_call(kernel, out_shape=jax.ShapeDtypeStruct(hidden.shape, hidde...]
where the time goes in v3:
time: 84.1 us; the launch traced here: 84 us
  Pallas kernels  81.6 us (97%)
  local copies, waits for them, and re-layouts  2.36 us (3%)
    pallas_call x1, Pallas kernels, shards(): pl.pallas_call(kernel, out_shape=jax.ShapeDtypeStruct(hidden.shape, hidde...  81.6 us
    unnamed x1, local copies, waits for them, and re-layouts  2.36 us

profile of v3, /device:TPU:1, one launch (start us, length us, event | category | flops | bytes accessed | tf_op | source)
XLA Modules:
  0.0 84.0 jit_solution(11955746663827148167)
XLA Ops:
  0.0 81.6 %attend.1 = bf16[2,96,3072]{2,1,0:T(8,128)(2,1)} custom-call(bf16[2,96,3072]{2,1,0:T(8,128)(2,1)} %hidden.1, bf16[2,96,1536]{2,1,0:T(8,128)(2,1)} %queries.1, bf16[2,96,1536]{2,1,0:T(8,128)(2,1)} %keys.1, bf16[2,96,1536]{2,1,0:T(8,128)(2,1)} %values.1, bf16[1536,3072]{1,0:T(8,128)(2,1)} %weight.1, f32[50,3072]{1,0:T(8,128)} %gates.1, s32[2]{0:T(128)} %steps.1), custom_call_target="tpu_custom_call" | custom-call | tf_op jit(solution)/shard_map/attend/pallas_call | solution.py:456
  81.6 2.4 %copy.9 = bf16[2,96,3072]{2,1,0:T(8,128)(2,1)} copy(bf16[2,96,3072]{2,1,0:T(8,128)(2,1)} %attend.1) | data formatting | bytes 2359296

commit v4 on v3

--- a/solution.py
+++ b/solution.py
@@ -52,8 +52,8 @@
     7: (((3, 3), 1, 1, 0), ((3, 1), 1, 3, 1)),
     8: (((2, 3), 1, 1, 0), ((2, 1), 1, 3, 1)),
 }
-HAND_ON = 10
-WITH_PARTNER = 10
+HAND_ON = 11
+WITH_PARTNER = 11
 
 
 def block_of(index):
@@ -277,7 +277,7 @@
             for step in range(2):
                 for n in range(CHUNK // HD):
                     start = step * CHUNK + n * HD
-                    scaled = q_in[q, s, step, n * HD:(n + 1) * HD, :].astype(jnp.float32).T * LOG2_SCALE
+                    scaled = q_in[q, s, step, n * HD:(n + 1) * HD, :].T.astype(jnp.float32) * LOG2_SCALE
                     high = scaled.astype(jnp.bfloat16)
                     qt[q, s, :HD, start:start + HD] = high
                     qt[q, s, HD:, start:start + HD] = (scaled - high.astype(jnp.float32)).astype(jnp.bfloat16)

time: 84.1 us -> 86.8 us (1.032)
  Pallas kernels: 81.6 us -> 84.2 us
    pallas_call x1, Pallas kernels: 81.6 us -> 84.2 us  [shards(): pl.pallas_call(kernel, out_shape=jax.ShapeDtypeStruct(hidden.shape, hidde...]
where the time goes in v4:
time: 86.8 us; the launch traced here: 86.5 us
  Pallas kernels  84.2 us (97%)
  local copies, waits for them, and re-layouts  2.36 us (3%)
    pallas_call x1, Pallas kernels, shards(): pl.pallas_call(kernel, out_shape=jax.ShapeDtypeStruct(hidden.shape, hidde...  84.2 us
    unnamed x1, local copies, waits for them, and re-layouts  2.36 us

profile of v4, /device:TPU:1, one launch (start us, length us, event | category | flops | bytes accessed | tf_op | source)
XLA Modules:
  0.0 86.5 jit_solution(445327694405675031)
XLA Ops:
  0.0 84.2 %attend.1 = bf16[2,96,3072]{2,1,0:T(8,128)(2,1)} custom-call(bf16[2,96,3072]{2,1,0:T(8,128)(2,1)} %hidden.1, bf16[2,96,1536]{2,1,0:T(8,128)(2,1)} %queries.1, bf16[2,96,1536]{2,1,0:T(8,128)(2,1)} %keys.1, bf16[2,96,1536]{2,1,0:T(8,128)(2,1)} %values.1, bf16[1536,3072]{1,0:T(8,128)(2,1)} %weight.1, f32[50,3072]{1,0:T(8,128)} %gates.1, s32[2]{0:T(128)} %steps.1), custom_call_target="tpu_custom_call" | custom-call | tf_op jit(solution)/shard_map/attend/pallas_call | solution.py:456
  84.2 2.4 %copy.9 = bf16[2,96,3072]{2,1,0:T(8,128)(2,1)} copy(bf16[2,96,3072]{2,1,0:T(8,128)(2,1)} %attend.1) | data formatting | bytes 2359296
